TPU v7x, 32 devices: a whole 2x2x4 slice. The times are simulated.
32 devices in a mesh: groups: 2 (over y), seq: 4 (over z), mp: 2 (over x), sub: 2 (over core).
Axes of the slice: x: 2, y: 2, z: 4, core: 2. Of those that a mesh axis runs over, the one named last changes fastest.
Arguments:
- video_in: bfloat16 [1024, 4096], P(('groups', 'seq'), ('mp', 'sub')), parts along dimension 0, may hold values from -6 to 6
- audio_in: bfloat16 [256, 2048], P(('groups', 'seq'), ('mp', 'sub')), parts along dimension 0, may hold values from -6 to 6
- q_self: bfloat16 [1024, 2048], P(('groups', 'seq'), ('mp', 'sub')), parts along dimension 0
- k_self: bfloat16 [1024, 2048], P(('groups', 'seq'), ('mp', 'sub')), parts along dimension 0
- v_self: bfloat16 [1024, 2048], P(('groups', 'seq'), ('mp', 'sub')), parts along dimension 0, may hold values from -6 to 6
- q_a2v: bfloat16 [1024, 1024], P(('groups', 'seq'), ('mp', 'sub')), parts along dimension 0
- k_a2v: bfloat16 [256, 1024], P(('groups', 'seq'), ('mp', 'sub')), parts along dimension 0
- v_a2v: bfloat16 [256, 1024], P(('groups', 'seq'), ('mp', 'sub')), parts along dimension 0, may hold values from -6 to 6
- q_v2a: bfloat16 [256, 1024], P(('groups', 'seq'), ('mp', 'sub')), parts along dimension 0
- k_v2a: bfloat16 [1024, 1024], P(('groups', 'seq'), ('mp', 'sub')), parts along dimension 0
- v_v2a: bfloat16 [1024, 1024], P(('groups', 'seq'), ('mp', 'sub')), parts along dimension 0, may hold values from -6 to 6
- wo_self: bfloat16 [2048, 4096], P(('mp', 'sub')), may hold values from -0.125 to 0.125
- wo_a2v: bfloat16 [1024, 4096], P(('mp', 'sub')), may hold values from -0.1875 to 0.1875
- wo_v2a: bfloat16 [1024, 2048], P(('mp', 'sub')), may hold values from -0.1875 to 0.1875
- video_gates: bfloat16 [16, 2, 4096], replicated, may hold values from -4 to 4
- audio_gates: bfloat16 [16, 2048], replicated, may hold values from -4 to 4
- video_steps: int32 [1024], P(('groups', 'seq')), parts along dimension 0, may hold values from 0 to 15
- audio_steps: int32 [256], P(('groups', 'seq')), parts along dimension 0, may hold values from 0 to 15
- audio_len: int32 [2], P('groups'), parts along dimension 0, may hold values from 64 to 128
Outputs:
- video_out: bfloat16 [1024, 4096], P(('groups', 'seq'), ('mp', 'sub')), parts along dimension 0
- audio_out: bfloat16 [256, 2048], P(('groups', 'seq'), ('mp', 'sub')), parts along dimension 0
There are 2 independent parts, one for each index of `groups`. A program takes and returns all parts, laid end to end along the dimension named above; an argument that names none is the same for every part. Nothing has to cross between parts.
Inputs may be any that keep to these rules, and one draw needn't show every extreme that they name: Audio tokens 0 to audio_len[0] - 1 are real, the rest are padding.
All inputs are finite; a program needn't handle non-finite values.
Results may differ from a plain program's by a relative error of at most 0.0075.
Values may be sent and summed in bfloat16 or wider, within the bound.
A program may use at most 64 MiB of HBM per device.

v0:
```python
import math

import jax
import jax.numpy as jnp
from jax import lax
from jax.sharding import PartitionSpec as P

DHV = 128
DHC = 64
NT = 16


def start_state(rows, heads, width):
    return (
        jnp.full((rows, heads), -1e30, jnp.float32),
        jnp.zeros((rows, heads), jnp.float32),
        jnp.zeros((rows, heads, width), jnp.float32),
    )


def update_block(state, queries, keys, values, heads, width, allowed):
    rows = queries.shape[0]
    count = keys.shape[0]
    q_heads = queries.reshape(rows, heads, width)
    k_heads = keys.reshape(count, heads, width)
    v_heads = values.reshape(count, heads, width)
    scores = jnp.einsum(
        "qhd,khd->qhk", q_heads, k_heads, preferred_element_type=jnp.float32
    ) / math.sqrt(width)
    if allowed is not None:
        scores = jnp.where(allowed[None, None, :], scores, -jnp.inf)
    peak_old, total_old, summed_old = state
    peak = jnp.maximum(peak_old, jnp.max(scores, axis=2))
    weights = jnp.exp(scores - peak[:, :, None])
    factor = jnp.exp(peak_old - peak)
    total = total_old * factor + jnp.sum(weights, axis=2)
    summed = summed_old * factor[:, :, None] + jnp.einsum(
        "qhk,khd->qhd", weights.astype(jnp.bfloat16), v_heads, preferred_element_type=jnp.float32
    )
    return (peak, total, summed)


def update_state(state, queries, keys, values, heads, width, start, limit):
    count = keys.shape[0]
    block = 1024 if count > 1024 and count % 1024 == 0 else count
    if block == count:
        allowed = None
        if limit is not None:
            allowed = jnp.arange(count, dtype=jnp.int32) < limit
        return update_block(state, queries, keys, values, heads, width, allowed)
    steps = count // block
    key_blocks = keys.reshape(steps, block, keys.shape[1])
    value_blocks = values.reshape(steps, block, values.shape[1])
    offsets = jnp.arange(steps, dtype=jnp.int32) * block

    def one_block(carry, items):
        key_rows, value_rows, offset = items
        allowed = None
        if limit is not None:
            allowed = start + offset + jnp.arange(block, dtype=jnp.int32) < limit
        return (update_block(carry, queries, key_rows, value_rows, heads, width, allowed), None)

    result, _ = lax.scan(one_block, state, (key_blocks, value_blocks, offsets))
    return result


def finish(state, heads, width):
    peak, total, summed = state
    rows = summed.shape[0]
    return (summed / total[:, :, None]).reshape(rows, heads * width).astype(jnp.bfloat16)


def on_device(
    video_in,
    audio_in,
    q_self,
    k_self,
    v_self,
    q_a2v,
    k_a2v,
    v_a2v,
    q_v2a,
    k_v2a,
    v_v2a,
    wo_self,
    wo_a2v,
    wo_v2a,
    video_gates,
    audio_gates,
    video_steps,
    audio_steps,
    audio_len,
):
    heads_self = q_self.shape[1] // DHV
    heads_cross = q_a2v.shape[1] // DHC
    rows_video = q_self.shape[0]
    rows_audio = q_v2a.shape[0]
    limit = audio_len[0]
    piece = (
        lax.all_gather(k_a2v, "seq", axis=0, tiled=True),
        lax.all_gather(v_a2v, "seq", axis=0, tiled=True),
    )
    a2v_state = update_state(
        start_state(rows_video, heads_cross, DHC),
        q_a2v,
        piece[0],
        piece[1],
        heads_cross,
        DHC,
        jnp.int32(0),
        limit,
    )
    a2v_att = finish(a2v_state, heads_cross, DHC)
    piece = (
        lax.all_gather(k_self, "seq", axis=0, tiled=True),
        lax.all_gather(v_self, "seq", axis=0, tiled=True),
    )
    self_state = update_state(
        start_state(rows_video, heads_self, DHV),
        q_self,
        piece[0],
        piece[1],
        heads_self,
        DHV,
        jnp.int32(0),
        None,
    )
    piece = (
        lax.all_gather(k_v2a, "seq", axis=0, tiled=True),
        lax.all_gather(v_v2a, "seq", axis=0, tiled=True),
    )
    v2a_state = update_state(
        start_state(rows_audio, heads_cross, DHC),
        q_v2a,
        piece[0],
        piece[1],
        heads_cross,
        DHC,
        jnp.int32(0),
        None,
    )
    self_att = finish(self_state, heads_self, DHV)
    v2a_att = finish(v2a_state, heads_cross, DHC)
    levels = jnp.arange(NT, dtype=jnp.int32)
    video_hot = (video_steps[:, None] == levels[None, :]).astype(jnp.bfloat16)
    video_gain = jnp.dot(video_hot, video_gates.reshape(NT, -1), preferred_element_type=jnp.float32)
    width_video = video_gates.shape[2]
    video_term = video_gain[:, :width_video] * jnp.dot(
        self_att, wo_self, preferred_element_type=jnp.float32
    )
    video_term = video_term + video_gain[:, width_video:] * jnp.dot(
        a2v_att, wo_a2v, preferred_element_type=jnp.float32
    )
    audio_hot = (audio_steps[:, None] == levels[None, :]).astype(jnp.bfloat16)
    audio_gain = jnp.dot(audio_hot, audio_gates, preferred_element_type=jnp.float32)
    positions = lax.axis_index("seq") * rows_audio + jnp.arange(rows_audio, dtype=jnp.int32)
    present = (positions < limit).astype(jnp.float32)
    audio_term = (
        present[:, None] * audio_gain * jnp.dot(v2a_att, wo_v2a, preferred_element_type=jnp.float32)
    )
    video_sum, audio_sum = (
        lax.psum_scatter(
            video_term.astype(jnp.bfloat16), ("mp", "sub"), scatter_dimension=1, tiled=True
        ).astype(jnp.float32),
        lax.psum_scatter(
            audio_term.astype(jnp.bfloat16), ("mp", "sub"), scatter_dimension=1, tiled=True
        ).astype(jnp.float32),
    )
    video_out = (video_in.astype(jnp.float32) + video_sum).astype(jnp.bfloat16)
    audio_out = (audio_in.astype(jnp.float32) + audio_sum).astype(jnp.bfloat16)
    return (video_out, audio_out)


def solution(mesh):
    in_specs = (
        P(("groups", "seq"), ("mp", "sub")),
        P(("groups", "seq"), ("mp", "sub")),
        P(("groups", "seq"), ("mp", "sub")),
        P(("groups", "seq"), ("mp", "sub")),
        P(("groups", "seq"), ("mp", "sub")),
        P(("groups", "seq"), ("mp", "sub")),
        P(("groups", "seq"), ("mp", "sub")),
        P(("groups", "seq"), ("mp", "sub")),
        P(("groups", "seq"), ("mp", "sub")),
        P(("groups", "seq"), ("mp", "sub")),
        P(("groups", "seq"), ("mp", "sub")),
        P(("mp", "sub"), None),
        P(("mp", "sub"), None),
        P(("mp", "sub"), None),
        P(),
        P(),
        P(("groups", "seq")),
        P(("groups", "seq")),
        P("groups"),
    )
    out_specs = (P(("groups", "seq"), ("mp", "sub")), P(("groups", "seq"), ("mp", "sub")))
    return jax.shard_map(
        on_device, mesh=mesh, in_specs=in_specs, out_specs=out_specs, check_vma=False
    )
```

profile of v0, /device:TPU:0, one launch (start us, length us, event | category | flops | bytes accessed | tf_op | source)
XLA Modules:
  0.0 149.2 jit_solution(6648957412750940869)
XLA Ops:
  8.0 16.0 %all_gather.22 = bf16[512,256]{1,0:T(8,128)(2,1)S(1)} all-gather(bf16[128,256]{1,0:T(8,128)(2,1)} %param.28), channel_id=1, replica_groups=mesh['groups'=2,'seq'=4,'mp'=2,'sub'=2] {'seq'}, dimensions={0}, use_global_device_ids=true | all-gather | bytes 327680 | tf_op jit(solution)/shard_map/all_gather | solution.py:129
  24.0 0.8 copy.40
  24.9 0.8 reshape.99
  25.7 1.2 fusion.39
  26.9 0.2 fusion.22
  27.1 0.5 copy-done.3
  27.6 0.6 exponential_multiply_fusion
  28.2 14.8 %all_gather.23 = bf16[512,256]{1,0:T(8,128)(2,1)S(1)} all-gather(bf16[128,256]{1,0:T(8,128)(2,1)} %param.29), channel_id=1, replica_groups=mesh['groups'=2,'seq'=4,'mp'=2,'sub'=2] {'seq'}, dimensions={0}, use_global_device_ids=true | all-gather | bytes 327680 | tf_op jit(solution)/shard_map/all_gather | solution.py:130
  42.9 0.8 copy.42
  43.8 1.3 fusion.15
  45.3 0.9 convolution_multiply_fusion.3
  46.2 1.0 fusion.2
  47.2 13.2 %all_gather.20 = bf16[128,256]{1,0:T(8,128)(2,1)S(1)} all-gather(bf16[32,256]{1,0:T(8,128)(2,1)S(1)} %copy-done.12), channel_id=1, replica_groups=mesh['groups'=2,'seq'=4,'mp'=2,'sub'=2] {'seq'}, dimensions={0}, use_global_device_ids=true | all-gather | bytes 81920 | tf_op jit(solution)/shard_map/all_gather | solution.py:100
  60.6 0.3 fusion.38
  61.0 13.3 %all_gather.21 = bf16[128,256]{1,0:T(8,128)(2,1)S(1)} all-gather(bf16[32,256]{1,0:T(8,128)(2,1)S(1)} %copy-done.13), channel_id=1, replica_groups=mesh['groups'=2,'seq'=4,'mp'=2,'sub'=2] {'seq'}, dimensions={0}, use_global_device_ids=true | all-gather | bytes 81920 | tf_op jit(solution)/shard_map/all_gather | solution.py:101
  74.4 0.7 copy.38
  75.2 15.5 %all_gather.18 = bf16[512,512]{0,1:T(8,128)(2,1)S(1)} all-gather(bf16[128,512]{0,1:T(8,128)(2,1)S(1)} %copy.31), channel_id=1, replica_groups=mesh['groups'=2,'seq'=4,'mp'=2,'sub'=2] {'seq'}, dimensions={0}, use_global_device_ids=true | all-gather | bytes 655360 | tf_op jit(solution)/shard_map/all_gather | solution.py:115
  90.8 1.3 fusion.37
  92.0 0.2 fusion.16
  92.2 0.6 exponential_multiply_fusion.2
  92.8 15.4 %all_gather.19 = bf16[512,512]{1,0:T(8,128)(2,1)} all-gather(bf16[128,512]{1,0:T(8,128)(2,1)S(1)} %copy-done.6), channel_id=1, replica_groups=mesh['groups'=2,'seq'=4,'mp'=2,'sub'=2] {'seq'}, dimensions={0}, use_global_device_ids=true | all-gather | bytes 655360 | tf_op jit(solution)/shard_map/all_gather | solution.py:116
  108.2 2.0 %copy.34 = bf16[512,512]{0,1:T(8,128)(2,1)} copy(bf16[512,512]{1,0:T(8,128)(2,1)} %all_gather.19) | data formatting | bytes 1048576 | tf_op jit(solution)/shard_map/all_gather | solution.py:116
  110.2 1.1 copy.48
  111.4 1.6 %fusion.30 = f32[128,8192]{1,0:T(8,128)S(1)} fusion(bf16[16,8192]{1,0:T(8,128)(2,1)S(1)} %bitcast.69, s32[128]{0:T(128)} %param.35), kind=kOutput, calls=%fused_computation.43 | convolution fusion | flops 33556480 | bytes 4456960 | tf_op jit(solution)/shard_map/dot_general | solution.py:146
  113.0 0.2 fusion.12
  113.2 0.3 fusion.9
  113.5 0.2 copy-done.1
  113.8 0.8 convolution_multiply_fusion.1
  114.6 1.6 %fusion.1 = bf16[128,4096]{1,0:T(8,128)(2,1)} fusion(f32[128,4096]{1,0:T(8,128)S(1)} %convolution_multiply_fusion.1, bf16[128,256]{0,1:T(8,128)(2,1)S(1)} %bitcast.77, bf16[256,4096]{1,0:T(8,128)(2,1)S(1)} %copy-done, f32[128,8192]{1,0:T(8,128)S(1)} %fusion.30), kind=kOutput, calls=%fused_computation.3 | convolution fusion | flops 270008320 | bytes 7405568 | tf_op jit(solution)/shard_map/dot_general | solution.py:151
  116.2 1.4 add_convert_fusion.1
  117.6 23.0 %reduce-scatter.3.cloned.1.call-done = bf16[128,1024]{1,0:T(8,128)(2,1)} async-done(((bf16[128,4096]{1,0:T(8,128)(2,1)}), bf16[128,1024]{1,0:T(8,128)(2,1)}) %reduce-scatter.3.cloned.1.call-update) | async-done | bytes 262160 | tf_op jit(solution)/shard_map/reduce_scatter | solution.py:162
  140.6 1.7 %add_convert_fusion = bf16[128,1024]{1,0:T(8,128)(2,1)} fusion(bf16[128,1024]{1,0:T(8,128)(2,1)} %reduce-scatter.3.cloned.1.call-done, bf16[128,1024]{1,0:T(8,128)(2,1)S(1)} %copy-done.5), kind=kLoop, calls=%fused_computation.29 | loop fusion | flops 524288 | bytes 786432 | tf_op jit(solution)/shard_map/convert_element_type | solution.py:169
  (49 shorter events, 0.8 us)
Async XLA Ops:
  7.2 107.4 %copy-start = (bf16[256,4096]{1,0:T(8,128)(2,1)S(1)}, bf16[256,4096]{1,0:T(8,128)(2,1)}, u32[]{:S(2)}) copy-start(bf16[256,4096]{1,0:T(8,128)(2,1)} %param.31) | copy-start | bytes 6291460
  7.2 38.1 %copy-start.8 = (bf16[16,2048]{1,0:T(8,128)(2,1)S(1)}, bf16[16,2048]{1,0:T(8,128)(2,1)}, u32[]{:S(2)}) copy-start(bf16[16,2048]{1,0:T(8,128)(2,1)} %param.34) | copy-start | bytes 196612
  7.2 39.0 %copy-start.2 = (bf16[256,2048]{1,0:T(8,128)(2,1)S(1)}, bf16[256,2048]{1,0:T(8,128)(2,1)}, u32[]{:S(2)}) copy-start(bf16[256,2048]{1,0:T(8,128)(2,1)} %param.32) | copy-start | bytes 3145732
  7.2 109.0 %reduce-scatter.5.cloned.1.call-start = ((), (), s32[]{:S(2)}) async-start(), calls=%async_computation.3 | async-start | bytes 163840 | tf_op jit(solution)/shard_map/reduce_scatter | solution.py:165
  25.7 21.6 %copy-start.12 = (bf16[32,256]{1,0:T(8,128)(2,1)S(1)}, bf16[32,256]{1,0:T(8,128)(2,1)}, u32[]{:S(2)}) copy-start(bf16[32,256]{1,0:T(8,128)(2,1)} %param.25) | copy-start | bytes 49156
  26.9 0.7 copy-start.3
  26.9 33.6 %copy-start.9 = (bf16[128,256]{1,0:T(8,128)(2,1)S(1)}, bf16[128,256]{1,0:T(8,128)(2,1)}, u32[]{:S(2)}) copy-start(bf16[128,256]{1,0:T(8,128)(2,1)} %param.24) | copy-start | bytes 196612
  26.9 0.7 copy-start.14
  43.8 17.2 %copy-start.13 = (bf16[32,256]{1,0:T(8,128)(2,1)S(1)}, bf16[32,256]{1,0:T(8,128)(2,1)}, u32[]{:S(2)}) copy-start(bf16[32,256]{1,0:T(8,128)(2,1)} %param.26) | copy-start | bytes 49156
  43.8 31.3 %copy-start.7 = (bf16[128,512]{1,0:T(8,128)(2,1)S(1)}, bf16[128,512]{1,0:T(8,128)(2,1)}, u32[]{:S(2)}) copy-start(bf16[128,512]{1,0:T(8,128)(2,1)} %param.22) | copy-start | bytes 393220
  47.2 93.4 %reduce-scatter.3.cloned.1.call-start = ((), (), s32[]{:S(2)}) async-start(), calls=%async_computation.2 | async-start | bytes 1310720 | tf_op jit(solution)/shard_map/reduce_scatter | solution.py:162
  60.9 31.9 %copy-start.6 = (bf16[128,512]{1,0:T(8,128)(2,1)S(1)}, bf16[128,512]{1,0:T(8,128)(2,1)}, u32[]{:S(2)}) copy-start(bf16[128,512]{1,0:T(8,128)(2,1)} %param.23) | copy-start | bytes 393220
  110.2 2.7 %copy-start.10 = (bf16[128,256]{0,1:T(8,128)(2,1)S(1)}, bf16[128,256]{0,1:T(8,128)(2,1)}, u32[]{:S(2)}) copy-start(bf16[128,256]{0,1:T(8,128)(2,1)} %copy.38) | copy-start | bytes 196612
  111.4 1.8 %copy-start.4 = (bf16[512,512]{0,1:T(8,128)(2,1)S(1)}, bf16[512,512]{0,1:T(8,128)(2,1)}, u32[]{:S(2)}) copy-start(bf16[512,512]{0,1:T(8,128)(2,1)} %copy.34) | copy-start | bytes 1572868
  111.4 1.8 %copy-start.15 = (f32[128,4]{0,1:T(4,128)S(1)}, f32[128,4]{0,1:T(4,128)}, u32[]{:S(2)}) copy-start(f32[128,4]{0,1:T(4,128)} %get-tuple-element.6) | copy-start | bytes 6148
  111.4 1.8 %copy-start.16 = (f32[128,4]{0,1:T(4,128)S(1)}, f32[128,4]{0,1:T(4,128)}, u32[]{:S(2)}) copy-start(f32[128,4]{0,1:T(4,128)} %get-tuple-element.7) | copy-start | bytes 6148
  111.4 2.4 %copy-start.1 = (bf16[512,4096]{1,0:T(8,128)(2,1)S(1)}, bf16[512,4096]{1,0:T(8,128)(2,1)}, u32[]{:S(2)}) copy-start(bf16[512,4096]{1,0:T(8,128)(2,1)} %param.30) | copy-start | bytes 12582916
  114.5 1.7 %copy-start.11 = (bf16[32,512]{1,0:T(8,128)(2,1)S(1)}, bf16[32,512]{1,0:T(8,128)(2,1)}, u32[]{:S(2)}) copy-start(bf16[32,512]{1,0:T(8,128)(2,1)} %param.20) | copy-start | bytes 98308
  114.5 26.1 %copy-start.5 = (bf16[128,1024]{1,0:T(8,128)(2,1)S(1)}, bf16[128,1024]{1,0:T(8,128)(2,1)}, u32[]{:S(2)}) copy-start(bf16[128,1024]{1,0:T(8,128)(2,1)} %param.19) | copy-start | bytes 786436
Sparse Core Ops, SparseCore 0:
  47.3 20.4 reduce-scatter.4
  116.3 24.2 reduce-scatter.2
where the time goes:
time: 150 us; the launch traced here: 149 us
  blocking collectives  88.2 us (59%)
  waiting for transfers between devices  23.1 us (15%)
  between operations  15.2 us (10%)
  matrix products  10.3 us (7%)
  local copies, waits for them, and re-layouts  7.66 us (5%)
  other arithmetic  4.72 us (3%)
    reduce_scatter x1, waiting for transfers between devices, on_device(): lax.psum_scatter(video_term.astype(jnp.bfloat16), ('mp', 'sub'), scatter_...  23 us
    all_gather x1, blocking collectives, on_device(): lax.all_gather(k_v2a, 'seq', axis=0, tiled=True)  16 us
    all_gather x1, blocking collectives, on_device(): lax.all_gather(k_self, 'seq', axis=0, tiled=True)  15.5 us
    all_gather x1, blocking collectives, on_device(): lax.all_gather(v_self, 'seq', axis=0, tiled=True)  15.4 us
    all_gather x1, blocking collectives, on_device(): lax.all_gather(v_v2a, 'seq', axis=0, tiled=True)  14.8 us
    all_gather x1, blocking collectives, on_device(): lax.all_gather(v_a2v, 'seq', axis=0, tiled=True)  13.3 us
    all_gather x1, blocking collectives, on_device(): lax.all_gather(k_a2v, 'seq', axis=0, tiled=True)  13.2 us
  transfers between devices with their start and end apart: 2, of which 1 were waited for; matrix products, arithmetic and copies ran while one was open for 8% of the time, Pallas kernels for 0%

commit v1 on v0

--- a/solution.py
+++ b/solution.py
@@ -1,8 +1,11 @@
+import functools
 import math
 
 import jax
 import jax.numpy as jnp
 from jax import lax
+from jax.experimental import pallas as pl
+from jax.experimental.pallas import tpu as pltpu
 from jax.sharding import PartitionSpec as P
 
 DHV = 128
@@ -70,7 +73,491 @@
     return (summed / total[:, :, None]).reshape(rows, heads * width).astype(jnp.bfloat16)
 
 
+MESH = pl.DeviceIdType.MESH
+BF16 = jnp.bfloat16
+F32 = jnp.float32
+CHUNKS = 4
+
+
+def fits(mesh, q_self, q_a2v, k_a2v):
+    seq = mesh.shape["seq"]
+    return (
+        seq > 1
+        and q_self.shape[1] == seq * DHV
+        and q_a2v.shape[1] == seq * DHC
+        and 2 * DHC == DHV
+        and seq % 2 == 0
+        and k_a2v.shape[0] % 32 == 0
+        and seq * q_self.shape[0] <= 1024
+        and mesh.shape["sub"] == 2
+        and mesh.shape["mp"] > 1
+    )
+
+
+def attend(queries, keys, values, width, allowed=None):
+    scores = lax.dot_general(
+        queries, keys, (((1,), (1,)), ((), ())), preferred_element_type=F32
+    )
+    if allowed is not None:
+        scores = jnp.where(allowed, scores, -jnp.inf)
+    peak = jnp.max(scores, axis=1, keepdims=True)
+    weights = jnp.exp2((scores - peak) * (math.log2(math.e) / math.sqrt(width)))
+    total = jnp.sum(weights, axis=1, keepdims=True)
+    summed = jnp.dot(weights.astype(BF16), values, preferred_element_type=F32)
+    return summed / total
+
+
+def spread(hot, table):
+    return lax.dot_general(hot, table, (((0,), (0,)), ((), ())), preferred_element_type=F32)
+
+
+def kernel(
+    seq,
+    mp,
+    video_in,
+    audio_in,
+    q_self,
+    k_self,
+    v_self,
+    q_a2v,
+    k_a2v,
+    v_a2v,
+    q_v2a,
+    k_v2a,
+    v_v2a,
+    wo_self,
+    wo_a2v,
+    wo_v2a,
+    video_gates,
+    audio_gates,
+    video_steps,
+    audio_steps,
+    audio_len,
+    video_out,
+    audio_out,
+    qs,
+    ks,
+    vs,
+    qa,
+    ka,
+    va,
+    qv_in,
+    kv_in,
+    vv_in,
+    q_pack,
+    kv_pack,
+    q_got,
+    kv_got,
+    os_send,
+    os,
+    ov_send,
+    ov_got,
+    ws,
+    wa,
+    wv,
+    vg,
+    ag,
+    vin,
+    ain,
+    gain,
+    term,
+    core_send,
+    core_got,
+    kept,
+    mp_send,
+    mp_got,
+    acore_send,
+    acore_got,
+    akept,
+    amp_send,
+    amp_got,
+    local_sem,
+    seq_send_sem,
+    seq_recv_sem,
+    core_send_sem,
+    core_recv_sem,
+    mp_send_sem,
+    mp_recv_sem,
+):
+    me = lax.axis_index("seq")
+    my_mp = lax.axis_index("mp")
+    my_sub = lax.axis_index("sub")
+    rows = q_self.shape[0]
+    arows = k_a2v.shape[0]
+    width_v = wo_self.shape[1]
+    width_a = wo_v2a.shape[1]
+    owned_v = width_v // (2 * mp)
+    owned_a = width_a // (2 * mp)
+    part = owned_v // CHUNKS
+
+    def at(index, size):
+        return pl.ds(pl.multiple_of(index * size, size), size)
+
+    def peer(d):
+        return lax.rem(me + d, seq)
+
+    def other_mp(d):
+        return lax.rem(my_mp + d, mp)
+
+    local = []
+
+    def bring(source, target):
+        copy = pltpu.make_async_copy(source, target, local_sem.at[len(local)])
+        copy.start()
+        local.append(copy)
+        return copy
+
+    cross = [
+        bring(q_v2a, qv_in),
+        bring(k_v2a, kv_in),
+        bring(v_v2a, vv_in),
+    ]
+    first = [
+        bring(video_gates, vg),
+        bring(q_a2v, qa),
+        bring(k_a2v, ka.at[at(me, arows)]),
+        bring(v_a2v, va.at[at(me, arows)]),
+        bring(wo_a2v, wa),
+    ]
+    own = [
+        bring(q_self.at[:, at(me, DHV)], qs.at[at(me, rows)]),
+        bring(k_self.at[:, at(me, DHV)], ks.at[at(me, rows)]),
+        bring(v_self.at[:, at(me, DHV)], vs.at[at(me, rows)]),
+    ]
+    late = [
+        bring(wo_self, ws),
+        bring(wo_v2a, wv),
+        bring(audio_gates, ag),
+        bring(video_in, vin),
+        bring(audio_in, ain),
+    ]
+
+    barrier = pltpu.get_barrier_semaphore()
+    for d in range(1, seq):
+        pl.semaphore_signal(barrier, inc=1, device_id={"seq": peer(d)}, device_id_type=MESH)
+    pl.semaphore_signal(barrier, inc=1, device_id={"sub": 1 - my_sub}, device_id_type=MESH)
+    for d in range(1, mp):
+        pl.semaphore_signal(barrier, inc=1, device_id={"mp": other_mp(d)}, device_id_type=MESH)
+    pl.semaphore_wait(barrier, seq - 1 + 1 + mp - 1)
+
+    sent = []
+
+    def to_seq(kind, d, source, target):
+        copy = pltpu.make_async_remote_copy(
+            src_ref=source,
+            dst_ref=target,
+            send_sem=seq_send_sem.at[kind, d],
+            recv_sem=seq_recv_sem.at[kind, d],
+            device_id={"seq": peer(d)},
+            device_id_type=MESH,
+        )
+        copy.start()
+        sent.append(copy)
+        return copy
+
+    order = [d for d in range(1, seq)]
+    self_in = []
+    for kind, (source, target) in enumerate(((k_self, ks), (q_self, qs), (v_self, vs))):
+        for d in order:
+            self_in.append(
+                to_seq(kind, d, source.at[:, at(peer(d), DHV)], target.at[at(me, rows)])
+            )
+    a2v_in = []
+    for kind, (source, target) in enumerate(((k_a2v, ka), (v_a2v, va))):
+        for d in order:
+            a2v_in.append(to_seq(3 + kind, d, source, target.at[at(me, arows)]))
+
+    for copy in cross:
+        copy.wait()
+    half = arows // 2
+    for h in range(seq):
+        cols = slice(h * DHC, (h + 1) * DHC)
+        kv = jnp.concatenate(
+            [kv_in[:, cols].astype(F32), vv_in[:, cols].astype(F32)], axis=1
+        ).astype(BF16)
+        qh = qv_in[:, cols].astype(F32)
+        kv_pack[h] = kv
+        q_pack[h] = jnp.concatenate([qh[:half], qh[half:]], axis=1).astype(BF16)
+    v2a_in = []
+    for d in order:
+        v2a_in.append(to_seq(5, d, q_pack.at[peer(d)], q_got.at[me]))
+        v2a_in.append(to_seq(6, d, kv_pack.at[peer(d)], kv_got.at[at(me, rows)]))
+    q_got[me] = q_pack[me]
+    kv_got[at(me, rows), :] = kv_pack[me]
+
+    for copy in first:
+        copy.wait()
+    levels2 = vg.shape[0]
+    picks = lax.broadcasted_iota(jnp.int32, (levels2, rows), 0)
+    steps2 = video_steps[...] * 2
+    hot_self = (picks == steps2).astype(F32).astype(BF16)
+    hot_a2v = (picks == steps2 + 1).astype(F32).astype(BF16)
+    tile = min(512, width_v)
+    for c in range(width_v // tile):
+        cols = slice(c * tile, (c + 1) * tile)
+        gain[:, cols] = spread(hot_self, vg[:, cols]).astype(BF16)
+    for copy in a2v_in:
+        copy.wait_recv()
+    count = seq * arows
+    limit = audio_len[0]
+    allowed = lax.broadcasted_iota(jnp.int32, (2 * rows, count), 1) < limit
+    low = lax.broadcasted_iota(jnp.int32, (rows, 2 * DHC), 1) < DHC
+    pieces = []
+    for pair in range(seq // 2):
+        cols = slice(pair * 2 * DHC, (pair + 1) * 2 * DHC)
+        qp = qa[:, cols]
+        zero = jnp.zeros_like(qp)
+        both = jnp.concatenate([jnp.where(low, qp, zero), jnp.where(low, zero, qp)], axis=0)
+        out = attend(both, ka[:, cols], va[:, cols], DHC, allowed)
+        pieces.append(jnp.where(low, out[:rows], out[rows:]).astype(BF16))
+    a2v_att = jnp.concatenate(pieces, axis=1)
+    for c in range(width_v // tile):
+        cols = slice(c * tile, (c + 1) * tile)
+        term[:, cols] = spread(hot_a2v, vg[:, cols]) * jnp.dot(
+            a2v_att, wa[:, cols], preferred_element_type=F32
+        )
+
+    for copy in own:
+        copy.wait()
+    for copy in self_in:
+        copy.wait_recv()
+    self_back = []
+    for d in order + [0]:
+        out = attend(qs[at(peer(d), rows), :], ks[...], vs[...], DHV).astype(BF16)
+        if d == 0:
+            os[:, at(me, DHV)] = out
+        else:
+            os_send[d] = out
+            self_back.append(to_seq(7, d, os_send.at[d], os.at[:, at(me, DHV)]))
+
+    for copy in v2a_in:
+        copy.wait_recv()
+    blocks = []
+    for p in range(seq):
+        got = q_got[p].astype(F32)
+        blocks.append(got[:, :DHC])
+        blocks.append(got[:, DHC:])
+    qv = jnp.concatenate(blocks, axis=0)
+    qv = jnp.concatenate([qv, jnp.zeros_like(qv)], axis=1).astype(BF16)
+    out = attend(qv, kv_got[...], kv_got[...], DHC)[:, DHC:]
+    for p in range(seq):
+        top = out[p * arows : p * arows + half]
+        bottom = out[p * arows + half : (p + 1) * arows]
+        ov_send[p] = jnp.concatenate([top, bottom], axis=1).astype(BF16)
+    v2a_back = []
+    for d in order:
+        v2a_back.append(to_seq(8, d, ov_send.at[peer(d)], ov_got.at[me]))
+    ov_got[me] = ov_send[me]
+
+    for copy in late:
+        copy.wait()
+    for copy in self_back:
+        copy.wait_recv()
+    self_att = os[...]
+
+    def owner(m, s):
+        return 2 * m + s
+
+    def video_part(m, s, c):
+        cols = pl.ds(pl.multiple_of(owner(m, s) * owned_v + c * part, part), part)
+        return term[:, cols] + gain[:, cols].astype(F32) * jnp.dot(
+            self_att, ws[:, cols], preferred_element_type=F32
+        )
+
+    def to_core(c, source, target):
+        copy = pltpu.make_async_remote_copy(
+            src_ref=source,
+            dst_ref=target,
+            send_sem=core_send_sem.at[c],
+            recv_sem=core_recv_sem.at[c],
+            device_id={"sub": 1 - my_sub},
+            device_id_type=MESH,
+        )
+        copy.start()
+        sent.append(copy)
+        return copy
+
+    def to_mp(c, d, source, target):
+        copy = pltpu.make_async_remote_copy(
+            src_ref=source,
+            dst_ref=target,
+            send_sem=mp_send_sem.at[c, d],
+            recv_sem=mp_recv_sem.at[c, d],
+            device_id={"mp": other_mp(d)},
+            device_id_type=MESH,
+        )
+        copy.start()
+        sent.append(copy)
+        return copy
+
+    core_copies = {}
+    mp_copies = {}
+
+    def pass_on(c):
+        core_copies[c].wait_recv()
+        for d in range(1, mp):
+            mp_send[c, d] = (kept[c, d] + core_got[c, d].astype(F32)).astype(BF16)
+            mp_copies[c, d] = to_mp(c, d, mp_send.at[c, d], mp_got.at[c, d])
+        kept[c, 0] = kept[c, 0] + core_got[c, 0].astype(F32)
+
+    for c in range(CHUNKS):
+        for d in range(mp):
+            core_send[c, d] = video_part(other_mp(d), 1 - my_sub, c).astype(BF16)
+        core_copies[c] = to_core(c, core_send.at[c], core_got.at[c])
+        for d in range(mp):
+            kept[c, d] = video_part(other_mp(d), my_sub, c)
+        if c > 0:
+            pass_on(c - 1)
+    pass_on(CHUNKS - 1)
+
+    for copy in v2a_back:
+        copy.wait_recv()
+    blocks = []
+    for h in range(seq):
+        got = ov_got[h].astype(F32)
+        blocks.append(jnp.concatenate([got[:, :DHC], got[:, DHC:]], axis=0))
+    v2a_att = jnp.concatenate(blocks, axis=1).astype(BF16)
+    apicks = lax.broadcasted_iota(jnp.int32, (ag.shape[0], arows), 0)
+    hot_audio = (apicks == audio_steps[...]).astype(F32).astype(BF16)
+    positions = me * arows + lax.broadcasted_iota(jnp.int32, (arows, owned_a), 0)
+    present = (positions < limit).astype(F32)
+
+    def audio_part(m, s):
+        cols = at(owner(m, s), owned_a)
+        return (
+            present
+            * spread(hot_audio, ag[:, cols])
+            * jnp.dot(v2a_att, wv[:, cols], preferred_element_type=F32)
+        )
+
+    for d in range(mp):
+        acore_send[d] = audio_part(other_mp(d), 1 - my_sub).astype(BF16)
+    acore = to_core(CHUNKS, acore_send, acore_got)
+    for d in range(mp):
+        akept[d] = audio_part(other_mp(d), my_sub)
+    acore.wait_recv()
+    for d in range(1, mp):
+        amp_send[d] = (akept[d] + acore_got[d].astype(F32)).astype(BF16)
+        mp_copies[CHUNKS, d] = to_mp(CHUNKS, d, amp_send.at[d], amp_got.at[d])
+
+    for c in range(CHUNKS):
+        cols = slice(c * part, (c + 1) * part)
+        total = kept[c, 0]
+        for d in range(1, mp):
+            mp_copies[c, d].wait_recv()
+            total = total + mp_got[c, d].astype(F32)
+        video_out[:, cols] = (vin[:, cols].astype(F32) + total).astype(BF16)
+    total = akept[0] + acore_got[0].astype(F32)
+    for d in range(1, mp):
+        mp_copies[CHUNKS, d].wait_recv()
+        total = total + amp_got[d].astype(F32)
+    audio_out[...] = (ain[...].astype(F32) + total).astype(BF16)
+    for copy in sent:
+        copy.wait_send()
+
+
+def fused(mesh, *args):
+    (
+        video_in,
+        audio_in,
+        q_self,
+        _,
+        _,
+        q_a2v,
+        k_a2v,
+        _,
+        q_v2a,
+        k_v2a,
+        _,
+        wo_self,
+        wo_a2v,
+        wo_v2a,
+        video_gates,
+        audio_gates,
+        video_steps,
+        audio_steps,
+        _,
+    ) = args
+    seq, mp = mesh.shape["seq"], mesh.shape["mp"]
+    rows, arows = q_self.shape[0], k_a2v.shape[0]
+    args = list(args)
+    levels = video_gates.shape[0]
+    table = video_gates.reshape(2 * levels, video_gates.shape[2])
+    args[14] = table
+    args[16] = video_steps.reshape(1, rows)
+    args[17] = audio_steps.reshape(1, arows)
+    part = video_in.shape[1] // CHUNKS
+    owned_a = audio_in.shape[1]
+
+    def buffer(*shape, dtype=BF16):
+        return pltpu.VMEM(shape, dtype)
+
+    like = lambda array: pltpu.VMEM(array.shape, array.dtype)
+    scratch = [
+        buffer(seq * rows, DHV),
+        buffer(seq * rows, DHV),
+        buffer(seq * rows, DHV),
+        like(q_a2v),
+        buffer(seq * arows, seq * DHC),
+        buffer(seq * arows, seq * DHC),
+        like(q_v2a),
+        like(k_v2a),
+        like(k_v2a),
+        buffer(seq, arows // 2, 2 * DHC),
+        buffer(seq, rows, 2 * DHC),
+        buffer(seq, arows // 2, 2 * DHC),
+        buffer(seq * rows, 2 * DHC),
+        buffer(seq, rows, DHV),
+        buffer(rows, seq * DHV),
+        buffer(seq, arows // 2, 2 * DHC),
+        buffer(seq, arows // 2, 2 * DHC),
+        like(wo_self),
+        like(wo_a2v),
+        like(wo_v2a),
+        like(table),
+        like(audio_gates),
+        like(video_in),
+        like(audio_in),
+        buffer(rows, wo_self.shape[1]),
+        buffer(rows, wo_self.shape[1], dtype=F32),
+        buffer(CHUNKS, mp, rows, part),
+        buffer(CHUNKS, mp, rows, part),
+        buffer(CHUNKS, mp, rows, part, dtype=F32),
+        buffer(CHUNKS, mp, rows, part),
+        buffer(CHUNKS, mp, rows, part),
+        buffer(mp, arows, owned_a),
+        buffer(mp, arows, owned_a),
+        buffer(mp, arows, owned_a, dtype=F32),
+        buffer(mp, arows, owned_a),
+        buffer(mp, arows, owned_a),
+        pltpu.SemaphoreType.DMA((16,)),
+        pltpu.SemaphoreType.DMA((9, seq)),
+        pltpu.SemaphoreType.DMA((9, seq)),
+        pltpu.SemaphoreType.DMA((CHUNKS + 1,)),
+        pltpu.SemaphoreType.DMA((CHUNKS + 1,)),
+        pltpu.SemaphoreType.DMA((CHUNKS + 1, mp)),
+        pltpu.SemaphoreType.DMA((CHUNKS + 1, mp)),
+    ]
+    anywhere = pl.BlockSpec(memory_space=pl.ANY)
+    vmem = pl.BlockSpec(memory_space=pltpu.VMEM)
+    smem = pl.BlockSpec(memory_space=pltpu.SMEM)
+    return pl.pallas_call(
+        functools.partial(kernel, seq, mp),
+        out_shape=(
+            jax.ShapeDtypeStruct(video_in.shape, video_in.dtype),
+            jax.ShapeDtypeStruct(audio_in.shape, audio_in.dtype),
+        ),
+        in_specs=[anywhere] * 16 + [vmem, vmem, smem],
+        out_specs=(vmem, vmem),
+        scratch_shapes=scratch,
+        compiler_params=pltpu.CompilerParams(
+            collective_id=0, has_side_effects=True, vmem_limit_bytes=40 * 1024 * 1024
+        ),
+    )(*args)
+
+
 def on_device(
+    mesh,
     video_in,
     audio_in,
     q_self,
@@ -91,6 +578,29 @@
     audio_steps,
     audio_len,
 ):
+    if fits(mesh, q_self, q_a2v, k_a2v):
+        return fused(
+            mesh,
+            video_in,
+            audio_in,
+            q_self,
+            k_self,
+            v_self,
+            q_a2v,
+            k_a2v,
+            v_a2v,
+            q_v2a,
+            k_v2a,
+            v_v2a,
+            wo_self,
+            wo_a2v,
+            wo_v2a,
+            video_gates,
+            audio_gates,
+            video_steps,
+            audio_steps,
+            audio_len,
+        )
     heads_self = q_self.shape[1] // DHV
     heads_cross = q_a2v.shape[1] // DHC
     rows_video = q_self.shape[0]
@@ -195,5 +705,5 @@
     )
     out_specs = (P(("groups", "seq"), ("mp", "sub")), P(("groups", "seq"), ("mp", "sub")))
     return jax.shard_map(
-        on_device, mesh=mesh, in_specs=in_specs, out_specs=out_specs, check_vma=False
-    )
+        functools.partial(on_device, mesh), mesh=mesh, in_specs=in_specs, out_specs=out_specs, check_vma=False
+    )

time: 150 us -> 58.4 us (0.39)
  blocking collectives: 88.2 us -> 0 us
  Pallas kernels: 0 us -> 37.7 us
  waiting for transfers between devices: 23.1 us -> 0 us
  between operations: 15.2 us -> 1.31 us
  local copies, waits for them, and re-layouts: 7.66 us -> 18.6 us
  matrix products: 10.3 us -> 0 us
  other arithmetic: 4.72 us -> 0 us
    all_gather x6 -> x0, blocking collectives: 88.2 us -> none  [the longest x1 16 us: on_device(): lax.all_gather(k_v2a, 'seq', axis=0, tiled=True)]
    pallas_call x0 -> x1, Pallas kernels: none -> 37.7 us  [fused(): pl.pallas_call(functools.partial(kernel, seq, mp), out_shape=(jax.ShapeDt...]
    reduce_scatter x2 -> x0, waiting for transfers between devices: 23 us -> none  [the longest x1 23 us: on_device(): lax.psum_scatter(video_term.astype(jnp.bfloat16), ('mp', 'sub'), scatter_...]
    unnamed x37 -> x36, local copies, waits for them, and re-layouts: 2.16 us -> 17.6 us
    dot_general x11 -> x0, matrix products: 10.3 us -> none  [the longest x3 2.72 us: update_block(): jnp.einsum('qhd,khd->qhk', q_heads, k_heads, preferred_element_type=jnp.f...]
    all_gather x5 -> x0, local copies, waits for them, and re-layouts: 4.57 us -> none  [the longest x1 2.04 us: on_device(): lax.all_gather(v_self, 'seq', axis=0, tiled=True)]
    convert_element_type x3 -> x0, other arithmetic: 3.11 us -> none  [the longest x1 1.72 us: on_device(): video_out = (video_in.astype(jnp.float32) + video_sum).astype(jnp.bfloat16)]
  transfers between devices with their start and end apart: 2 -> 0, of which waited for: 1 -> 0; matrix products, arithmetic and copies ran while one was open for 8% -> 0% of each run, Pallas kernels for 0% -> 0%
where the time goes in v1:
time: 58.4 us; the launch traced here: 57.6 us
  Pallas kernels  37.7 us (65%)
  local copies, waits for them, and re-layouts  18.6 us (32%)
  between operations  1.31 us (2%)
    pallas_call x1, Pallas kernels, fused(): pl.pallas_call(functools.partial(kernel, seq, mp), out_shape=(jax.ShapeDt...  37.7 us
    unnamed x36, local copies, waits for them, and re-layouts  17.6 us

profile of v1, /device:TPU:0, one launch (start us, length us, event | category | flops | bytes accessed | tf_op | source)
XLA Modules:
  0.0 57.6 jit_solution(3091990483806988299)
XLA Ops:
  1.3 1.0 %reshape.13.video_gates = bf16[32,4096]{1,0:T(8,128)(2,1)S(1)} reshape(bf16[16,2,4096]{2,1,0:T(2,128)(2,1)} %param.33) | data formatting | bytes 524288 | tf_op jit(solution)/shard_map/reshape | solution.py:485
  2.3 0.0 copy-start
  2.3 2.2 %copy-done = bf16[512,4096]{1,0:T(8,128)(2,1)S(1)} copy-done((bf16[512,4096]{1,0:T(8,128)(2,1)S(1)}, bf16[512,4096]{1,0:T(8,128)(2,1)}, u32[]{:S(2)}) %copy-start) | copy-done | bytes 4194328
  4.5 0.0 copy-start.1
  4.5 1.6 %copy-done.1 = bf16[256,4096]{1,0:T(8,128)(2,1)S(1)} copy-done((bf16[256,4096]{1,0:T(8,128)(2,1)S(1)}, bf16[256,4096]{1,0:T(8,128)(2,1)}, u32[]{:S(2)}) %copy-start.1) | copy-done | bytes 2097176
  6.1 0.0 copy-start.2
  6.1 1.2 %copy-done.2 = bf16[256,2048]{1,0:T(8,128)(2,1)S(1)} copy-done((bf16[256,2048]{1,0:T(8,128)(2,1)S(1)}, bf16[256,2048]{1,0:T(8,128)(2,1)}, u32[]{:S(2)}) %copy-start.2) | copy-done | bytes 1048600
  7.3 0.0 copy-start.3
  7.3 0.9 %copy-done.3 = bf16[128,1024]{1,0:T(8,128)(2,1)S(1)} copy-done((bf16[128,1024]{1,0:T(8,128)(2,1)S(1)}, bf16[128,1024]{1,0:T(8,128)(2,1)}, u32[]{:S(2)}) %copy-start.3) | copy-done | bytes 262168
  8.3 0.0 copy-start.4
  8.3 0.9 %copy-done.4 = bf16[128,512]{1,0:T(8,128)(2,1)S(1)} copy-done((bf16[128,512]{1,0:T(8,128)(2,1)S(1)}, bf16[128,512]{1,0:T(8,128)(2,1)}, u32[]{:S(2)}) %copy-start.4) | copy-done | bytes 131096
  9.2 0.9 %copy-done.5 = bf16[128,512]{1,0:T(8,128)(2,1)S(1)} copy-done((bf16[128,512]{1,0:T(8,128)(2,1)S(1)}, bf16[128,512]{1,0:T(8,128)(2,1)}, u32[]{:S(2)}) %copy-start.5) | copy-done | bytes 131096
  10.1 0.0 copy-start.6
  10.1 0.9 %copy-done.6 = bf16[128,512]{1,0:T(8,128)(2,1)S(1)} copy-done((bf16[128,512]{1,0:T(8,128)(2,1)S(1)}, bf16[128,512]{1,0:T(8,128)(2,1)}, u32[]{:S(2)}) %copy-start.6) | copy-done | bytes 131096
  11.0 0.0 copy-start.7
  11.0 0.8 %copy-done.7 = bf16[128,256]{1,0:T(8,128)(2,1)S(1)} copy-done((bf16[128,256]{1,0:T(8,128)(2,1)S(1)}, bf16[128,256]{1,0:T(8,128)(2,1)}, u32[]{:S(2)}) %copy-start.7) | copy-done | bytes 65560
  11.8 0.0 copy-start.8
  11.8 0.8 %copy-done.8 = bf16[128,256]{1,0:T(8,128)(2,1)S(1)} copy-done((bf16[128,256]{1,0:T(8,128)(2,1)S(1)}, bf16[128,256]{1,0:T(8,128)(2,1)}, u32[]{:S(2)}) %copy-start.8) | copy-done | bytes 65560
  12.7 0.0 copy-start.9
  12.7 0.8 %copy-done.9 = bf16[128,256]{1,0:T(8,128)(2,1)S(1)} copy-done((bf16[128,256]{1,0:T(8,128)(2,1)S(1)}, bf16[128,256]{1,0:T(8,128)(2,1)}, u32[]{:S(2)}) %copy-start.9) | copy-done | bytes 65560
  13.5 0.0 copy-start.10
  13.5 0.8 %copy-done.10 = bf16[16,2048]{1,0:T(8,128)(2,1)S(1)} copy-done((bf16[16,2048]{1,0:T(8,128)(2,1)S(1)}, bf16[16,2048]{1,0:T(8,128)(2,1)}, u32[]{:S(2)}) %copy-start.10) | copy-done | bytes 65560
  14.4 0.0 copy-start.11
  14.4 0.8 %copy-done.11 = bf16[32,512]{1,0:T(8,128)(2,1)S(1)} copy-done((bf16[32,512]{1,0:T(8,128)(2,1)S(1)}, bf16[32,512]{1,0:T(8,128)(2,1)}, u32[]{:S(2)}) %copy-start.11) | copy-done | bytes 32792
  15.1 0.7 %copy-done.12 = bf16[32,256]{1,0:T(8,128)(2,1)S(1)} copy-done((bf16[32,256]{1,0:T(8,128)(2,1)S(1)}, bf16[32,256]{1,0:T(8,128)(2,1)}, u32[]{:S(2)}) %copy-start.12) | copy-done | bytes 16408
  15.8 0.7 %copy-done.13 = bf16[32,256]{1,0:T(8,128)(2,1)S(1)} copy-done((bf16[32,256]{1,0:T(8,128)(2,1)S(1)}, bf16[32,256]{1,0:T(8,128)(2,1)}, u32[]{:S(2)}) %copy-start.13) | copy-done | bytes 16408
  16.6 0.7 %copy-done.14 = bf16[32,256]{1,0:T(8,128)(2,1)S(1)} copy-done((bf16[32,256]{1,0:T(8,128)(2,1)S(1)}, bf16[32,256]{1,0:T(8,128)(2,1)}, u32[]{:S(2)}) %copy-start.14) | copy-done | bytes 16408
  17.3 0.7 %copy-done.15 = s32[128]{0:T(128)S(1)} copy-done((s32[128]{0:T(128)S(1)}, s32[128]{0:T(128)}, u32[]{:S(2)}) %copy-start.15) | copy-done | bytes 536
  17.9 0.7 %copy-done.16 = s32[32]{0:T(128)S(1)} copy-done((s32[32]{0:T(128)S(1)}, s32[32]{0:T(128)}, u32[]{:S(2)}) %copy-start.16) | copy-done | bytes 152
  18.6 37.7 %shard_map.194 = (bf16[128,1024]{1,0:T(8,128)(2,1)S(1)}, bf16[32,512]{1,0:T(8,128)(2,1)S(1)}) custom-call(bf16[128,1024]{1,0:T(8,128)(2,1)S(1)} %copy-done.3, bf16[32,512]{1,0:T(8,128)(2,1)S(1)} %copy-done.11, bf16[128,512]{1,0:T(8,128)(2,1)S(1)} %copy-done.4, bf16[128,512]{1,0:T(8,128)(2,1)S(1)} %copy-done.5, bf16[128,512]{1,0:T(8,128)(2,1)S(1)} %copy-done.6, ...), custom_call_target="tpu_custom_call" | custom-call | tf_op jit(solution)/shard_map/pallas_call | solution.py:544
  56.3 0.7 %copy.24 = bf16[128,1024]{1,0:T(8,128)(2,1)} copy(bf16[128,1024]{1,0:T(8,128)(2,1)S(1)} %get-tuple-element.4) | data formatting | bytes 524288
  57.0 0.6 %copy.25 = bf16[32,512]{1,0:T(8,128)(2,1)} copy(bf16[32,512]{1,0:T(8,128)(2,1)S(1)} %get-tuple-element.5) | data formatting | bytes 65536
  (6 shorter events, 0.0 us)
Async XLA Ops:
  2.3 2.2 %copy-start = (bf16[512,4096]{1,0:T(8,128)(2,1)S(1)}, bf16[512,4096]{1,0:T(8,128)(2,1)}, u32[]{:S(2)}) copy-start(bf16[512,4096]{1,0:T(8,128)(2,1)} %wo_self.1) | copy-start | bytes 12582916
  4.5 1.6 %copy-start.1 = (bf16[256,4096]{1,0:T(8,128)(2,1)S(1)}, bf16[256,4096]{1,0:T(8,128)(2,1)}, u32[]{:S(2)}) copy-start(bf16[256,4096]{1,0:T(8,128)(2,1)} %wo_a2v.1) | copy-start | bytes 6291460
  6.1 1.2 %copy-start.2 = (bf16[256,2048]{1,0:T(8,128)(2,1)S(1)}, bf16[256,2048]{1,0:T(8,128)(2,1)}, u32[]{:S(2)}) copy-start(bf16[256,2048]{1,0:T(8,128)(2,1)} %wo_v2a.1) | copy-start | bytes 3145732
  7.3 0.9 %copy-start.3 = (bf16[128,1024]{1,0:T(8,128)(2,1)S(1)}, bf16[128,1024]{1,0:T(8,128)(2,1)}, u32[]{:S(2)}) copy-start(bf16[128,1024]{1,0:T(8,128)(2,1)} %video_in.1) | copy-start | bytes 786436
  8.3 0.9 %copy-start.4 = (bf16[128,512]{1,0:T(8,128)(2,1)S(1)}, bf16[128,512]{1,0:T(8,128)(2,1)}, u32[]{:S(2)}) copy-start(bf16[128,512]{1,0:T(8,128)(2,1)} %q_self.1) | copy-start | bytes 393220
  9.2 0.9 %copy-start.5 = (bf16[128,512]{1,0:T(8,128)(2,1)S(1)}, bf16[128,512]{1,0:T(8,128)(2,1)}, u32[]{:S(2)}) copy-start(bf16[128,512]{1,0:T(8,128)(2,1)} %k_self.1) | copy-start | bytes 393220
  10.1 0.9 %copy-start.6 = (bf16[128,512]{1,0:T(8,128)(2,1)S(1)}, bf16[128,512]{1,0:T(8,128)(2,1)}, u32[]{:S(2)}) copy-start(bf16[128,512]{1,0:T(8,128)(2,1)} %v_self.1) | copy-start | bytes 393220
  11.0 0.8 %copy-start.7 = (bf16[128,256]{1,0:T(8,128)(2,1)S(1)}, bf16[128,256]{1,0:T(8,128)(2,1)}, u32[]{:S(2)}) copy-start(bf16[128,256]{1,0:T(8,128)(2,1)} %q_a2v.1) | copy-start | bytes 196612
  11.8 0.8 %copy-start.8 = (bf16[128,256]{1,0:T(8,128)(2,1)S(1)}, bf16[128,256]{1,0:T(8,128)(2,1)}, u32[]{:S(2)}) copy-start(bf16[128,256]{1,0:T(8,128)(2,1)} %k_v2a.1) | copy-start | bytes 196612
  12.7 0.8 %copy-start.9 = (bf16[128,256]{1,0:T(8,128)(2,1)S(1)}, bf16[128,256]{1,0:T(8,128)(2,1)}, u32[]{:S(2)}) copy-start(bf16[128,256]{1,0:T(8,128)(2,1)} %v_v2a.1) | copy-start | bytes 196612
  13.5 0.8 %copy-start.10 = (bf16[16,2048]{1,0:T(8,128)(2,1)S(1)}, bf16[16,2048]{1,0:T(8,128)(2,1)}, u32[]{:S(2)}) copy-start(bf16[16,2048]{1,0:T(8,128)(2,1)} %audio_gates.1) | copy-start | bytes 196612
  14.4 0.8 %copy-start.11 = (bf16[32,512]{1,0:T(8,128)(2,1)S(1)}, bf16[32,512]{1,0:T(8,128)(2,1)}, u32[]{:S(2)}) copy-start(bf16[32,512]{1,0:T(8,128)(2,1)} %audio_in.1) | copy-start | bytes 98308
  15.1 0.7 %copy-start.12 = (bf16[32,256]{1,0:T(8,128)(2,1)S(1)}, bf16[32,256]{1,0:T(8,128)(2,1)}, u32[]{:S(2)}) copy-start(bf16[32,256]{1,0:T(8,128)(2,1)} %k_a2v.1) | copy-start | bytes 49156
  15.8 0.7 %copy-start.13 = (bf16[32,256]{1,0:T(8,128)(2,1)S(1)}, bf16[32,256]{1,0:T(8,128)(2,1)}, u32[]{:S(2)}) copy-start(bf16[32,256]{1,0:T(8,128)(2,1)} %v_a2v.1) | copy-start | bytes 49156
  16.6 0.7 %copy-start.14 = (bf16[32,256]{1,0:T(8,128)(2,1)S(1)}, bf16[32,256]{1,0:T(8,128)(2,1)}, u32[]{:S(2)}) copy-start(bf16[32,256]{1,0:T(8,128)(2,1)} %q_v2a.1) | copy-start | bytes 49156
  17.3 0.7 %copy-start.15 = (s32[128]{0:T(128)S(1)}, s32[128]{0:T(128)}, u32[]{:S(2)}) copy-start(s32[128]{0:T(128)} %param.35) | copy-start | bytes 1540
  17.9 0.7 %copy-start.16 = (s32[32]{0:T(128)S(1)}, s32[32]{0:T(128)}, u32[]{:S(2)}) copy-start(s32[32]{0:T(128)} %param.36) | copy-start | bytes 388

commit v2 on v1

--- a/solution.py
+++ b/solution.py
@@ -159,6 +159,11 @@
     ag,
     vin,
     ain,
+    vsteps,
+    asteps,
+    alen,
+    vout,
+    aout,
     gain,
     term,
     core_send,
@@ -213,6 +218,8 @@
         bring(v_v2a, vv_in),
     ]
     first = [
+        bring(video_steps, vsteps),
+        bring(audio_len, alen),
         bring(video_gates, vg),
         bring(q_a2v, qa),
         bring(k_a2v, ka.at[at(me, arows)]),
@@ -228,6 +235,7 @@
         bring(wo_self, ws),
         bring(wo_v2a, wv),
         bring(audio_gates, ag),
+        bring(audio_steps, asteps),
         bring(video_in, vin),
         bring(audio_in, ain),
     ]
@@ -287,19 +295,16 @@
 
     for copy in first:
         copy.wait()
-    levels2 = vg.shape[0]
-    picks = lax.broadcasted_iota(jnp.int32, (levels2, rows), 0)
-    steps2 = video_steps[...] * 2
-    hot_self = (picks == steps2).astype(F32).astype(BF16)
-    hot_a2v = (picks == steps2 + 1).astype(F32).astype(BF16)
+    picks = lax.broadcasted_iota(jnp.int32, (vg.shape[0], rows), 0)
+    hot = (picks == vsteps[...]).astype(F32).astype(BF16)
     tile = min(512, width_v)
     for c in range(width_v // tile):
         cols = slice(c * tile, (c + 1) * tile)
-        gain[:, cols] = spread(hot_self, vg[:, cols]).astype(BF16)
+        gain[:, cols] = spread(hot, vg[:, 0, cols]).astype(BF16)
     for copy in a2v_in:
         copy.wait_recv()
     count = seq * arows
-    limit = audio_len[0]
+    limit = alen[0]
     allowed = lax.broadcasted_iota(jnp.int32, (2 * rows, count), 1) < limit
     low = lax.broadcasted_iota(jnp.int32, (rows, 2 * DHC), 1) < DHC
     pieces = []
@@ -313,7 +318,7 @@
     a2v_att = jnp.concatenate(pieces, axis=1)
     for c in range(width_v // tile):
         cols = slice(c * tile, (c + 1) * tile)
-        term[:, cols] = spread(hot_a2v, vg[:, cols]) * jnp.dot(
+        term[:, cols] = spread(hot, vg[:, 1, cols]) * jnp.dot(
             a2v_att, wa[:, cols], preferred_element_type=F32
         )
 
@@ -418,7 +423,7 @@
         blocks.append(jnp.concatenate([got[:, :DHC], got[:, DHC:]], axis=0))
     v2a_att = jnp.concatenate(blocks, axis=1).astype(BF16)
     apicks = lax.broadcasted_iota(jnp.int32, (ag.shape[0], arows), 0)
-    hot_audio = (apicks == audio_steps[...]).astype(F32).astype(BF16)
+    hot_audio = (apicks == asteps[...]).astype(F32).astype(BF16)
     positions = me * arows + lax.broadcasted_iota(jnp.int32, (arows, owned_a), 0)
     present = (positions < limit).astype(F32)
 
@@ -440,18 +445,23 @@
         amp_send[d] = (akept[d] + acore_got[d].astype(F32)).astype(BF16)
         mp_copies[CHUNKS, d] = to_mp(CHUNKS, d, amp_send.at[d], amp_got.at[d])
 
+    results = []
     for c in range(CHUNKS):
         cols = slice(c * part, (c + 1) * part)
         total = kept[c, 0]
         for d in range(1, mp):
             mp_copies[c, d].wait_recv()
             total = total + mp_got[c, d].astype(F32)
-        video_out[:, cols] = (vin[:, cols].astype(F32) + total).astype(BF16)
+        vout[:, cols] = (vin[:, cols].astype(F32) + total).astype(BF16)
+        results.append(bring(vout.at[:, cols], video_out.at[:, cols]))
     total = akept[0] + acore_got[0].astype(F32)
     for d in range(1, mp):
         mp_copies[CHUNKS, d].wait_recv()
         total = total + amp_got[d].astype(F32)
-    audio_out[...] = (ain[...].astype(F32) + total).astype(BF16)
+    aout[...] = (ain[...].astype(F32) + total).astype(BF16)
+    results.append(bring(aout, audio_out))
+    for copy in results:
+        copy.wait()
     for copy in sent:
         copy.wait_send()
 
@@ -481,9 +491,6 @@
     seq, mp = mesh.shape["seq"], mesh.shape["mp"]
     rows, arows = q_self.shape[0], k_a2v.shape[0]
     args = list(args)
-    levels = video_gates.shape[0]
-    table = video_gates.reshape(2 * levels, video_gates.shape[2])
-    args[14] = table
     args[16] = video_steps.reshape(1, rows)
     args[17] = audio_steps.reshape(1, arows)
     part = video_in.shape[1] // CHUNKS
@@ -514,8 +521,13 @@
         like(wo_self),
         like(wo_a2v),
         like(wo_v2a),
-        like(table),
+        like(video_gates),
         like(audio_gates),
+        like(video_in),
+        like(audio_in),
+        buffer(1, rows, dtype=jnp.int32),
+        buffer(1, arows, dtype=jnp.int32),
+        pltpu.SMEM((1,), jnp.int32),
         like(video_in),
         like(audio_in),
         buffer(rows, wo_self.shape[1]),
@@ -530,7 +542,7 @@
         buffer(mp, arows, owned_a, dtype=F32),
         buffer(mp, arows, owned_a),
         buffer(mp, arows, owned_a),
-        pltpu.SemaphoreType.DMA((16,)),
+        pltpu.SemaphoreType.DMA((32,)),
         pltpu.SemaphoreType.DMA((9, seq)),
         pltpu.SemaphoreType.DMA((9, seq)),
         pltpu.SemaphoreType.DMA((CHUNKS + 1,)),
@@ -538,20 +550,18 @@
         pltpu.SemaphoreType.DMA((CHUNKS + 1, mp)),
         pltpu.SemaphoreType.DMA((CHUNKS + 1, mp)),
     ]
-    anywhere = pl.BlockSpec(memory_space=pl.ANY)
-    vmem = pl.BlockSpec(memory_space=pltpu.VMEM)
-    smem = pl.BlockSpec(memory_space=pltpu.SMEM)
+    anywhere = pl.BlockSpec(memory_space=pltpu.HBM)
     return pl.pallas_call(
         functools.partial(kernel, seq, mp),
         out_shape=(
             jax.ShapeDtypeStruct(video_in.shape, video_in.dtype),
             jax.ShapeDtypeStruct(audio_in.shape, audio_in.dtype),
         ),
-        in_specs=[anywhere] * 16 + [vmem, vmem, smem],
-        out_specs=(vmem, vmem),
+        in_specs=[anywhere] * len(args),
+        out_specs=(anywhere, anywhere),
         scratch_shapes=scratch,
         compiler_params=pltpu.CompilerParams(
-            collective_id=0, has_side_effects=True, vmem_limit_bytes=40 * 1024 * 1024
+            collective_id=0, has_side_effects=True, vmem_limit_bytes=63 * 1024 * 1024
         ),
     )(*args)
 

time: 58.4 us -> 42.3 us (0.72); the launches traced: 57.6 us -> 42.1 us
  local copies, waits for them, and re-layouts: 18.6 us -> 3.04 us
    unnamed x36 -> x2, local copies, waits for them, and re-layouts: 17.6 us -> 3.04 us
    reshape x1 -> x0, local copies, waits for them, and re-layouts: 1.05 us -> none  [fused(): table = video_gates.reshape(2 * levels, video_gates.shape[2])]
where the time goes in v2:
time: 42.3 us; the launch traced here: 42.1 us
  Pallas kernels  37.8 us (89%)
  local copies, waits for them, and re-layouts  3.04 us (7%)
  between operations  1.29 us (3%)
    pallas_call x1, Pallas kernels, fused(): pl.pallas_call(functools.partial(kernel, seq, mp), out_shape=(jax.ShapeDt...  37.8 us
    unnamed x2, local copies, waits for them, and re-layouts  3.04 us

profile of v2, /device:TPU:0, one launch (start us, length us, event | category | flops | bytes accessed | tf_op | source)
XLA Modules:
  0.0 42.1 jit_solution(18349746903652068460)
XLA Ops:
  1.3 37.8 %shard_map.194 = (bf16[128,1024]{1,0:T(8,128)(2,1)}, bf16[32,512]{1,0:T(8,128)(2,1)}) custom-call(bf16[128,1024]{1,0:T(8,128)(2,1)} %video_in.1, bf16[32,512]{1,0:T(8,128)(2,1)} %audio_in.1, bf16[128,512]{1,0:T(8,128)(2,1)} %q_self.1, bf16[128,512]{1,0:T(8,128)(2,1)} %k_self.1, bf16[128,512]{1,0:T(8,128)(2,1)} %v_self.1, bf16[128,256]{1,0:T(8,128)(2,1)} %q_a2v.1, ...), custom_call_target="tpu_custom_call" | custom-call | tf_op jit(solution)/shard_map/pallas_call | solution.py:554
  39.0 1.7 %copy.24 = bf16[128,1024]{1,0:T(8,128)(2,1)} copy(bf16[128,1024]{1,0:T(8,128)(2,1)} %get-tuple-element.4) | data formatting | bytes 524288
  40.7 1.4 %copy.25 = bf16[32,512]{1,0:T(8,128)(2,1)} copy(bf16[32,512]{1,0:T(8,128)(2,1)} %get-tuple-element.5) | data formatting | bytes 65536

commit v3 on v2

--- a/solution.py
+++ b/solution.py
@@ -76,7 +76,7 @@
 MESH = pl.DeviceIdType.MESH
 BF16 = jnp.bfloat16
 F32 = jnp.float32
-CHUNKS = 4
+CHUNKS = 2
 
 
 def fits(mesh, q_self, q_a2v, k_a2v):
@@ -286,10 +286,6 @@
         qh = qv_in[:, cols].astype(F32)
         kv_pack[h] = kv
         q_pack[h] = jnp.concatenate([qh[:half], qh[half:]], axis=1).astype(BF16)
-    v2a_in = []
-    for d in order:
-        v2a_in.append(to_seq(5, d, q_pack.at[peer(d)], q_got.at[me]))
-        v2a_in.append(to_seq(6, d, kv_pack.at[peer(d)], kv_got.at[at(me, rows)]))
     q_got[me] = q_pack[me]
     kv_got[at(me, rows), :] = kv_pack[me]
 
@@ -301,6 +297,24 @@
     for c in range(width_v // tile):
         cols = slice(c * tile, (c + 1) * tile)
         gain[:, cols] = spread(hot, vg[:, 0, cols]).astype(BF16)
+    for copy in own:
+        copy.wait()
+    for copy in self_in:
+        copy.wait_recv()
+    self_back = []
+    for d in order + [0]:
+        out = attend(qs[at(peer(d), rows), :], ks[...], vs[...], DHV).astype(BF16)
+        if d == 0:
+            os[:, at(me, DHV)] = out
+        else:
+            os_send[d] = out
+            self_back.append(to_seq(7, d, os_send.at[d], os.at[:, at(me, DHV)]))
+
+    v2a_in = []
+    for d in order:
+        v2a_in.append(to_seq(5, d, q_pack.at[peer(d)], q_got.at[me]))
+        v2a_in.append(to_seq(6, d, kv_pack.at[peer(d)], kv_got.at[at(me, rows)]))
+
     for copy in a2v_in:
         copy.wait_recv()
     count = seq * arows
@@ -322,18 +336,67 @@
             a2v_att, wa[:, cols], preferred_element_type=F32
         )
 
-    for copy in own:
+    for copy in late:
         copy.wait()
-    for copy in self_in:
+    for copy in self_back:
         copy.wait_recv()
-    self_back = []
-    for d in order + [0]:
-        out = attend(qs[at(peer(d), rows), :], ks[...], vs[...], DHV).astype(BF16)
-        if d == 0:
-            os[:, at(me, DHV)] = out
-        else:
-            os_send[d] = out
-            self_back.append(to_seq(7, d, os_send.at[d], os.at[:, at(me, DHV)]))
+    self_att = os[...]
+
+    def owner(m, s):
+        return 2 * m + s
+
+    def video_part(m, s, c):
+        cols = pl.ds(pl.multiple_of(owner(m, s) * owned_v + c * part, part), part)
+        return term[:, cols] + gain[:, cols].astype(F32) * jnp.dot(
+            self_att, ws[:, cols], preferred_element_type=F32
+        )
+
+    def to_core(c, d, source, target):
+        copy = pltpu.make_async_remote_copy(
+            src_ref=source,
+            dst_ref=target,
+            send_sem=core_send_sem.at[c, d],
+            recv_sem=core_recv_sem.at[c, d],
+            device_id={"sub": 1 - my_sub},
+            device_id_type=MESH,
+        )
+        copy.start()
+        sent.append(copy)
+        return copy
+
+    def to_mp(c, d, source, target):
+        copy = pltpu.make_async_remote_copy(
+            src_ref=source,
+            dst_ref=target,
+            send_sem=mp_send_sem.at[c, d],
+            recv_sem=mp_recv_sem.at[c, d],
+            device_id={"mp": other_mp(d)},
+            device_id_type=MESH,
+        )
+        copy.start()
+        sent.append(copy)
+        return copy
+
+    core_copies = {}
+    mp_copies = {}
+
+    def exchange(c, d):
+        core_send[c, d] = video_part(other_mp(d), 1 - my_sub, c).astype(BF16)
+        core_copies[c, d] = to_core(c, d, core_send.at[c, d], core_got.at[c, d])
+        kept[c, d] = video_part(other_mp(d), my_sub, c)
+
+    def pass_on(c):
+        for d in range(1, mp):
+            core_copies[c, d].wait_recv()
+            mp_send[c, d] = (kept[c, d] + core_got[c, d].astype(F32)).astype(BF16)
+            mp_copies[c, d] = to_mp(c, d, mp_send.at[c, d], mp_got.at[c, d])
+
+    for c in range(CHUNKS):
+        for d in range(1, mp):
+            exchange(c, d)
+        if c > 0:
+            pass_on(c - 1)
+    pass_on(CHUNKS - 1)
 
     for copy in v2a_in:
         copy.wait_recv()
@@ -354,66 +417,8 @@
         v2a_back.append(to_seq(8, d, ov_send.at[peer(d)], ov_got.at[me]))
     ov_got[me] = ov_send[me]
 
-    for copy in late:
-        copy.wait()
-    for copy in self_back:
-        copy.wait_recv()
-    self_att = os[...]
-
-    def owner(m, s):
-        return 2 * m + s
-
-    def video_part(m, s, c):
-        cols = pl.ds(pl.multiple_of(owner(m, s) * owned_v + c * part, part), part)
-        return term[:, cols] + gain[:, cols].astype(F32) * jnp.dot(
-            self_att, ws[:, cols], preferred_element_type=F32
-        )
-
-    def to_core(c, source, target):
-        copy = pltpu.make_async_remote_copy(
-            src_ref=source,
-            dst_ref=target,
-            send_sem=core_send_sem.at[c],
-            recv_sem=core_recv_sem.at[c],
-            device_id={"sub": 1 - my_sub},
-            device_id_type=MESH,
-        )
-        copy.start()
-        sent.append(copy)
-        return copy
-
-    def to_mp(c, d, source, target):
-        copy = pltpu.make_async_remote_copy(
-            src_ref=source,
-            dst_ref=target,
-            send_sem=mp_send_sem.at[c, d],
-            recv_sem=mp_recv_sem.at[c, d],
-            device_id={"mp": other_mp(d)},
-            device_id_type=MESH,
-        )
-        copy.start()
-        sent.append(copy)
-        return copy
-
-    core_copies = {}
-    mp_copies = {}
-
-    def pass_on(c):
-        core_copies[c].wait_recv()
-        for d in range(1, mp):
-            mp_send[c, d] = (kept[c, d] + core_got[c, d].astype(F32)).astype(BF16)
-            mp_copies[c, d] = to_mp(c, d, mp_send.at[c, d], mp_got.at[c, d])
-        kept[c, 0] = kept[c, 0] + core_got[c, 0].astype(F32)
-
     for c in range(CHUNKS):
-        for d in range(mp):
-            core_send[c, d] = video_part(other_mp(d), 1 - my_sub, c).astype(BF16)
-        core_copies[c] = to_core(c, core_send.at[c], core_got.at[c])
-        for d in range(mp):
-            kept[c, d] = video_part(other_mp(d), my_sub, c)
-        if c > 0:
-            pass_on(c - 1)
-    pass_on(CHUNKS - 1)
+        exchange(c, 0)
 
     for copy in v2a_back:
         copy.wait_recv()
@@ -437,7 +442,7 @@
 
     for d in range(mp):
         acore_send[d] = audio_part(other_mp(d), 1 - my_sub).astype(BF16)
-    acore = to_core(CHUNKS, acore_send, acore_got)
+    acore = to_core(CHUNKS, 0, acore_send, acore_got)
     for d in range(mp):
         akept[d] = audio_part(other_mp(d), my_sub)
     acore.wait_recv()
@@ -448,7 +453,8 @@
     results = []
     for c in range(CHUNKS):
         cols = slice(c * part, (c + 1) * part)
-        total = kept[c, 0]
+        core_copies[c, 0].wait_recv()
+        total = kept[c, 0] + core_got[c, 0].astype(F32)
         for d in range(1, mp):
             mp_copies[c, d].wait_recv()
             total = total + mp_got[c, d].astype(F32)
@@ -545,8 +551,8 @@
         pltpu.SemaphoreType.DMA((32,)),
         pltpu.SemaphoreType.DMA((9, seq)),
         pltpu.SemaphoreType.DMA((9, seq)),
-        pltpu.SemaphoreType.DMA((CHUNKS + 1,)),
-        pltpu.SemaphoreType.DMA((CHUNKS + 1,)),
+        pltpu.SemaphoreType.DMA((CHUNKS + 1, mp)),
+        pltpu.SemaphoreType.DMA((CHUNKS + 1, mp)),
         pltpu.SemaphoreType.DMA((CHUNKS + 1, mp)),
         pltpu.SemaphoreType.DMA((CHUNKS + 1, mp)),
     ]

time: 42.3 us -> 39.1 us (0.924)
  Pallas kernels: 37.8 us -> 34.5 us
    pallas_call x1, Pallas kernels: 37.8 us -> 34.5 us  [fused(): pl.pallas_call(functools.partial(kernel, seq, mp), out_shape=(jax.ShapeDt...]
where the time goes in v3:
time: 39.1 us; the launch traced here: 38.9 us
  Pallas kernels  34.5 us (88%)
  local copies, waits for them, and re-layouts  3.04 us (8%)
  between operations  1.29 us (3%)
    pallas_call x1, Pallas kernels, fused(): pl.pallas_call(functools.partial(kernel, seq, mp), out_shape=(jax.ShapeDt...  34.5 us
    unnamed x2, local copies, waits for them, and re-layouts  3.04 us

profile of v3, /device:TPU:0, one launch (start us, length us, event | category | flops | bytes accessed | tf_op | source)
XLA Modules:
  0.0 38.9 jit_solution(6407141328472510739)
XLA Ops:
  1.3 34.5 %shard_map.194 = (bf16[128,1024]{1,0:T(8,128)(2,1)}, bf16[32,512]{1,0:T(8,128)(2,1)}) custom-call(bf16[128,1024]{1,0:T(8,128)(2,1)} %video_in.1, bf16[32,512]{1,0:T(8,128)(2,1)} %audio_in.1, bf16[128,512]{1,0:T(8,128)(2,1)} %q_self.1, bf16[128,512]{1,0:T(8,128)(2,1)} %k_self.1, bf16[128,512]{1,0:T(8,128)(2,1)} %v_self.1, bf16[128,256]{1,0:T(8,128)(2,1)} %q_a2v.1, ...), custom_call_target="tpu_custom_call" | custom-call | tf_op jit(solution)/shard_map/pallas_call | solution.py:560
  35.8 1.7 %copy.24 = bf16[128,1024]{1,0:T(8,128)(2,1)} copy(bf16[128,1024]{1,0:T(8,128)(2,1)} %get-tuple-element.4) | data formatting | bytes 524288
  37.5 1.4 %copy.25 = bf16[32,512]{1,0:T(8,128)(2,1)} copy(bf16[32,512]{1,0:T(8,128)(2,1)} %get-tuple-element.5) | data formatting | bytes 65536

commit v4 on v3

--- a/solution.py
+++ b/solution.py
@@ -76,7 +76,7 @@
 MESH = pl.DeviceIdType.MESH
 BF16 = jnp.bfloat16
 F32 = jnp.float32
-CHUNKS = 2
+CHUNKS = 1
 
 
 def fits(mesh, q_self, q_a2v, k_a2v):
@@ -310,10 +310,6 @@
             os_send[d] = out
             self_back.append(to_seq(7, d, os_send.at[d], os.at[:, at(me, DHV)]))
 
-    v2a_in = []
-    for d in order:
-        v2a_in.append(to_seq(5, d, q_pack.at[peer(d)], q_got.at[me]))
-        v2a_in.append(to_seq(6, d, kv_pack.at[peer(d)], kv_got.at[at(me, rows)]))
 
     for copy in a2v_in:
         copy.wait_recv()
@@ -335,6 +331,11 @@
         term[:, cols] = spread(hot, vg[:, 1, cols]) * jnp.dot(
             a2v_att, wa[:, cols], preferred_element_type=F32
         )
+
+    v2a_in = []
+    for d in order:
+        v2a_in.append(to_seq(5, d, q_pack.at[peer(d)], q_got.at[me]))
+        v2a_in.append(to_seq(6, d, kv_pack.at[peer(d)], kv_got.at[at(me, rows)]))
 
     for copy in late:
         copy.wait()

time: 39.1 us -> 39.1 us (level)
  no operation moved by 1% of the time
where the time goes in v4:
time: 39.1 us; the launch traced here: 38.8 us
  Pallas kernels  34.5 us (88%)
  local copies, waits for them, and re-layouts  3.04 us (8%)
  between operations  1.29 us (3%)
    pallas_call x1, Pallas kernels, fused(): pl.pallas_call(functools.partial(kernel, seq, mp), out_shape=(jax.ShapeDt...  34.5 us
    unnamed x2, local copies, waits for them, and re-layouts  3.04 us

profile of v4, /device:TPU:0, one launch (start us, length us, event | category | flops | bytes accessed | tf_op | source)
XLA Modules:
  0.0 38.8 jit_solution(15912734227414979025)
XLA Ops:
  1.3 34.5 %shard_map.194 = (bf16[128,1024]{1,0:T(8,128)(2,1)}, bf16[32,512]{1,0:T(8,128)(2,1)}) custom-call(bf16[128,1024]{1,0:T(8,128)(2,1)} %video_in.1, bf16[32,512]{1,0:T(8,128)(2,1)} %audio_in.1, bf16[128,512]{1,0:T(8,128)(2,1)} %q_self.1, bf16[128,512]{1,0:T(8,128)(2,1)} %k_self.1, bf16[128,512]{1,0:T(8,128)(2,1)} %v_self.1, bf16[128,256]{1,0:T(8,128)(2,1)} %q_a2v.1, ...), custom_call_target="tpu_custom_call" | custom-call | tf_op jit(solution)/shard_map/pallas_call | solution.py:561
  35.8 1.7 %copy.24 = bf16[128,1024]{1,0:T(8,128)(2,1)} copy(bf16[128,1024]{1,0:T(8,128)(2,1)} %get-tuple-element.4) | data formatting | bytes 524288
  37.5 1.4 %copy.25 = bf16[32,512]{1,0:T(8,128)(2,1)} copy(bf16[32,512]{1,0:T(8,128)(2,1)} %get-tuple-element.5) | data formatting | bytes 65536
